TPU v7x, 256 devices: a whole 4x4x8 slice. The times are simulated.
256 devices in a mesh: row: 16 (over y_lo, z), col: 16 (over x, y_hi, core).
Axes of the slice: x: 4, y: 4 (y_hi: 2, y_lo: 2; y = y_hi * 2 + y_lo), z: 8, core: 2. Of those that a mesh axis runs over, the one named last changes fastest.
Arguments:
- features: bfloat16 [131072, 256], P(('col', 'row')), may hold values from -6 to 6
- weight: bfloat16 [256, 256], replicated, may hold values from -0.375 to 0.375
- cotangent: bfloat16 [131072, 256], P(('row', 'col')), may hold values from -6 to 6
- tiles: bfloat16 [16, 16, 32, 128, 128], P('row', 'col'), as said below
- coords: int32 [16, 16, 2, 32], P('row', 'col'), may hold values from 0 to 63, as said below
Outputs:
- activated: bfloat16 [131072, 256], P(('row', 'col'))
- feature_grad: bfloat16 [131072, 256], P(('col', 'row'))
- weight_grad: float32 [256, 256], replicated
Inputs may be any that keep to these rules, and one draw needn't show every extreme that they name: `coords`: each device's tiles lie at distinct positions. `tiles`: entries are zero or positive edge weights.
All inputs are finite; a program needn't handle non-finite values.
Results may differ from a plain program's by a relative error of at most 0.0061.
Values may be sent and summed in bfloat16 or wider, within the bound.
A program may use at most 128 MiB of HBM per device.

v0:
```python
import math

import jax
import jax.numpy as jnp
from jax import lax
from jax.sharding import PartitionSpec as P


def aggregate(blocks, targets, sources, source_rows, totals, flip):
    count = blocks.shape[0]
    group = math.gcd(count, 32)
    steps_total = count // group
    width = blocks.shape[1]
    stacks = (
        blocks.reshape(steps_total, group, width, width),
        targets.reshape(steps_total, group),
        sources.reshape(steps_total, group),
    )

    def advance(carry, item):
        blocks_now, target_now, source_now = item
        picked = source_rows[source_now]
        if flip:
            products = jnp.einsum(
                "gba,gbf->gaf", blocks_now, picked, preferred_element_type=jnp.float32
            )
        else:
            products = jnp.einsum(
                "gab,gbf->gaf", blocks_now, picked, preferred_element_type=jnp.float32
            )
        return (carry.at[target_now].add(products), None)

    carry, unused = lax.scan(advance, totals, stacks)
    return carry


def slope_of(pre):
    sigma = jax.nn.sigmoid(pre)
    return sigma * (1.0 + pre * (1.0 - sigma))


def body(features, weight, cotangent, tiles, coords):
    row_devices = lax.axis_size("row")
    col_devices = lax.axis_size("col")
    nodes_here, width = features.shape
    side = tiles.shape[-1]
    tile_here = tiles.shape[2]
    blocks = tiles.reshape(tile_here, side, side)
    row_ids = coords[0, 0, 0]
    col_ids = coords[0, 0, 1]
    row_count = nodes_here * col_devices // side
    col_count = nodes_here * row_devices // side
    column_group = lax.all_gather(features, "row", axis=0, tiled=True).reshape(
        col_count, side, width
    )
    forward = aggregate(
        blocks,
        row_ids,
        col_ids,
        column_group,
        jnp.zeros((row_count, side, width), jnp.float32),
        False,
    )
    forward = forward.reshape(row_count * side, width)
    own_agg = lax.psum_scatter(forward, "col", scatter_dimension=0, tiled=True).astype(jnp.bfloat16)
    own_pre = jnp.dot(own_agg, weight, preferred_element_type=jnp.float32)
    activated = jax.nn.silu(own_pre).astype(jnp.bfloat16)
    own_dpre = (cotangent.astype(jnp.float32) * slope_of(own_pre)).astype(jnp.bfloat16)
    own_dagg = jnp.dot(own_dpre, weight.T, preferred_element_type=jnp.float32).astype(jnp.bfloat16)
    dagg_rows = lax.all_gather(own_dagg, "col", axis=0, tiled=True)
    partial_weight = jnp.dot(own_agg.T, own_dpre, preferred_element_type=jnp.float32)
    backward = aggregate(
        blocks,
        col_ids,
        row_ids,
        dagg_rows.reshape(row_count, side, width),
        jnp.zeros((col_count, side, width), jnp.float32),
        True,
    )
    backward = backward.reshape(col_count * side, width)
    feature_grad = lax.psum_scatter(backward, "row", scatter_dimension=0, tiled=True).astype(
        jnp.bfloat16
    )
    weight_grad = lax.psum(partial_weight, ("row", "col"))
    return (activated, feature_grad, weight_grad)


def solution(mesh):
    return jax.shard_map(
        body,
        mesh=mesh,
        in_specs=(
            P(("col", "row"), None),
            P(),
            P(("row", "col"), None),
            P("row", "col", None, None, None),
            P("row", "col", None, None),
        ),
        out_specs=(P(("row", "col"), None), P(("col", "row"), None), P()),
        check_vma=False,
    )
```

profile of v0, /device:TPU:1, one launch (start us, length us, event | category | flops | bytes accessed | tf_op | source)
XLA Modules:
  0.0 673.5 jit_solution(16673128613769396629)
XLA Ops:
  7.2 0.0 copy-start
  7.2 0.0 all-gather.3.cloned.1.call-start
  7.2 0.7 all-gather.3.cloned.1.call-update
  7.9 0.0 reduce-scatter.3.cloned.1.call-start
  8.0 0.8 fusion.7
  8.7 73.0 %all-gather.3.cloned.1.call-done = bf16[8192,256]{1,0:T(8,128)(2,1)} async-done(((bf16[512,256]{1,0:T(8,128)(2,1)}), bf16[8192,256]{1,0:T(8,128)(2,1)}) %all-gather.3.cloned.1.call-update) | async-done | bytes 4194320 | tf_op jit(solution)/shard_map/all_gather | solution.py:53
  81.7 2.9 gather_fusion
  84.6 0.0 copy-done
  84.6 2.7 convolution_bitcast_fusion.1
  87.3 5.6 copy.11
  92.9 4.3 broadcast.46.clone
  97.1 9.9 %scatter_fusion = f32[64,128,256]{2,1,0:T(8,128)} fusion(f32[64,128,256]{2,1,0:T(8,128)} %broadcast.46.clone, s32[32]{0:T(128)S(1)} %get-tuple-element.36, f32[32,128,256]{2,1,0:T(8,128)} %copy.11), kind=kCustom, calls=%fused_computation.2 | custom fusion | flops 1048576 | bytes 12583040 | tf_op jit(solution)/shard_map/while/body/eval_jaxpr/scatter-add | solution.py:31
  107.1 0.0 copy-start.2
  107.1 0.0 copy-start.3
  107.1 0.0 reduce-scatter.3.cloned.1.call-update
  107.1 0.0 all-gather.5.cloned.1.call-start
  107.2 115.5 %reduce-scatter.3.cloned.1.call-done = f32[512,256]{1,0:T(8,128)} async-done(((f32[8192,256]{1,0:T(8,128)}), f32[512,256]{1,0:T(8,128)}) %reduce-scatter.3.cloned.1.call-update) | async-done | bytes 524304 | tf_op jit(solution)/shard_map/reduce_scatter | solution.py:65
  222.6 0.0 copy-done.2
  222.6 0.0 copy-done.3
  222.7 2.1 multiply_convert_fusion
  224.8 1.0 convolution_convert_fusion
  225.8 0.0 all-gather.5.cloned.1.call-update
  225.8 0.0 reduce-scatter.5.cloned.1.call-start
  225.8 61.7 %all-gather.5.cloned.1.call-done = bf16[8192,256]{1,0:T(8,128)(2,1)} async-done(((bf16[512,256]{1,0:T(8,128)(2,1)}), bf16[8192,256]{1,0:T(8,128)(2,1)}) %all-gather.5.cloned.1.call-update) | async-done | bytes 4194320 | tf_op jit(solution)/shard_map/all_gather | solution.py:70
  287.6 2.9 gather_fusion.1
  290.4 2.7 convolution_bitcast_fusion
  293.1 5.6 copy.13
  298.8 4.3 broadcast.46
  303.0 10.0 %scatter_fusion.1 = f32[64,128,256]{2,1,0:T(8,128)} fusion(f32[64,128,256]{2,1,0:T(8,128)} %broadcast.46, s32[32]{0:T(128)S(1)} %get-tuple-element.29, f32[32,128,256]{2,1,0:T(8,128)} %copy.13), kind=kCustom, calls=%fused_computation.3 | custom fusion | flops 1048576 | bytes 12583040 | tf_op jit(solution)/shard_map/while/body/eval_jaxpr/scatter-add | solution.py:31
  313.0 0.0 copy-start.1
  313.0 0.0 reduce-scatter.5.cloned.1.call-update
  313.1 0.0 all-reduce.2.cloned.1.call-start
  313.1 1.0 copy-done.1
  314.1 1.0 fusion.2
  315.0 0.0 all-reduce.2.cloned.1.call-update
  315.1 97.8 %reduce-scatter.5.cloned.1.call-done = f32[512,256]{1,0:T(8,128)} async-done(((f32[8192,256]{1,0:T(8,128)}), f32[512,256]{1,0:T(8,128)}) %reduce-scatter.5.cloned.1.call-update) | async-done | bytes 524304 | tf_op jit(solution)/shard_map/reduce_scatter | solution.py:81
  412.9 1.8 convert_element_type.23
  414.6 250.7 %all-reduce.2.cloned.1.call-done = f32[256,256]{1,0:T(8,128)} async-done(((f32[256,256]{1,0:T(8,128)}), f32[256,256]{1,0:T(8,128)}) %all-reduce.2.cloned.1.call-update) | async-done | bytes 262160 | tf_op jit(solution)/shard_map/psum | solution.py:84
  665.3 1.7 copy.19
  (2 shorter events, 0.0 us)
Async XLA Ops:
  7.2 77.4 %copy-start = (bf16[1,1,32,128,128]{4,3,2,1,0:T(8,128)(2,1)S(1)}, bf16[1,1,32,128,128]{4,3,2,1,0:T(8,128)(2,1)}, u32[]{:S(2)}) copy-start(bf16[1,1,32,128,128]{4,3,2,1,0:T(8,128)(2,1)} %param.8) | copy-start | bytes 3145732
  7.2 74.5 %all-gather.3.cloned.1.call-start = ((), (), s32[]{:S(2)}) async-start(), calls=%async_computation.2 | async-start | bytes 4456448 | tf_op jit(solution)/shard_map/all_gather | solution.py:53
  7.9 214.7 %reduce-scatter.3.cloned.1.call-start = ((), (), s32[]{:S(2)}) async-start(), calls=%async_computation.3 | async-start | bytes 8912896 | tf_op jit(solution)/shard_map/reduce_scatter | solution.py:65
  107.1 115.6 %copy-start.2 = (bf16[256,256]{1,0:T(8,128)(2,1)S(1)}, bf16[256,256]{1,0:T(8,128)(2,1)}, u32[]{:S(2)}) copy-start(bf16[256,256]{1,0:T(8,128)(2,1)} %param.6) | copy-start | bytes 393220
  107.1 115.6 %copy-start.3 = (bf16[512,256]{1,0:T(8,128)(2,1)S(1)}, bf16[512,256]{1,0:T(8,128)(2,1)}, u32[]{:S(2)}) copy-start(bf16[512,256]{1,0:T(8,128)(2,1)} %param.7) | copy-start | bytes 786436
  107.1 180.5 %all-gather.5.cloned.1.call-start = ((), (), s32[]{:S(2)}) async-start(), calls=%async_computation.4 | async-start | bytes 4456448 | tf_op jit(solution)/shard_map/all_gather | solution.py:70
  225.8 187.1 %reduce-scatter.5.cloned.1.call-start = ((), (), s32[]{:S(2)}) async-start(), calls=%async_computation.5 | async-start | bytes 8912896 | tf_op jit(solution)/shard_map/reduce_scatter | solution.py:81
  313.0 1.0 copy-start.1
  313.1 352.3 %all-reduce.2.cloned.1.call-start = ((), (), s32[]{:S(2)}) async-start(), calls=%async_computation.6 | async-start | bytes 524288 | tf_op jit(solution)/shard_map/psum | solution.py:84
Sparse Core Ops, SparseCore 0:
  9.8 71.8 all-gather.2
  107.2 115.3 reduce-scatter.2
  225.9 61.6 all-gather.4
  313.2 99.6 reduce-scatter.4
  418.7 246.5 all-reduce.1
where the time goes:
time: 675 us; the launch traced here: 674 us
  waiting for transfers between devices  599 us (89%)
  local copies, waits for them, and re-layouts  28.1 us (4%)
  other arithmetic  22.5 us (3%)
  between operations  13.8 us (2%)
  matrix products  9.48 us (1%)
    psum x1, waiting for transfers between devices, body(): weight_grad = lax.psum(partial_weight, ('row', 'col'))  251 us
    reduce_scatter x1, waiting for transfers between devices, body(): lax.psum_scatter(forward, 'col', scatter_dimension=0, tiled=True)  115 us
    reduce_scatter x1, waiting for transfers between devices, body(): lax.psum_scatter(backward, 'row', scatter_dimension=0, tiled=True)  97.8 us
    all_gather x1, waiting for transfers between devices, body(): lax.all_gather(features, 'row', axis=0, tiled=True)  73 us
    all_gather x1, waiting for transfers between devices, body(): dagg_rows = lax.all_gather(own_dagg, 'col', axis=0, tiled=True)  61.7 us
    scatter-add x2, other arithmetic, advance(): return (carry.at[target_now].add(products), None)  20 us
  transfers between devices with their start and end apart: 5, of which 5 were waited for; matrix products, arithmetic and copies ran while one was open for 1% of the time, Pallas kernels for 0%

commit v1 on v0

v1 whole, which is shorter than its diff:
```python
import jax
import jax.numpy as jnp
from jax import lax
from jax.experimental import pallas as pl
from jax.experimental.pallas import tpu as pltpu
from jax.sharding import PartitionSpec as P

MESH = pl.DeviceIdType.MESH
BF = jnp.bfloat16
F32 = jnp.float32
TB = 128
NT = 32
NZ = 8
NX = 4
SLOTS = NT + 1
SEMS = 192


def dot(a, b, da, db):
    return lax.dot_general(a, b, (((da,), (db,)), ((), ())), preferred_element_type=F32)


class Net:
    def __init__(self, send, recv):
        self.send, self.recv, self.used, self.started = send, recv, 0, []

    def copy(self, src, dst, device):
        c = pltpu.make_async_remote_copy(
            src_ref=src,
            dst_ref=dst,
            send_sem=self.send.at[self.used],
            recv_sem=self.recv.at[self.used],
            device_id=device,
            device_id_type=MESH,
        )
        self.used += 1
        c.start()
        self.started.append(c)
        return c

    def finish(self):
        for c in self.started:
            c.wait_send()


def wrap(v, n):
    return lax.rem(v + n, n)


def gather(net, n, k, p, dev, own, slot, fill):
    m = n // 2

    def origin(d, s):
        return wrap(k - s, n) if d == 0 else wrap(k + s, n)

    def side(d):
        return dev(wrap(k + 1, n) if d == 0 else wrap(k - 1, n), p)

    def ring(g, pp, d, s, src=None):
        o = origin(d, s - 1)
        lo, cnt = (0, 4) if s < m else (2 * d, 2)
        src = slot(g, pp, o, lo, cnt) if src is None else src
        return net.copy(src, slot(g, pp, o, lo, cnt), side(d))

    def across(o, lo, cnt, src=None):
        src = slot(1, p, o, lo, cnt) if src is None else src
        return net.copy(src, slot(1, p, o, lo, cnt), dev(k, 1 - p))

    q = 1 - p
    ya = net.copy(own(0), slot(0, p, k, 0, 4), dev(k, q))
    b = [ring(1, p, d, 1, own(1)) for d in (0, 1)]
    a0 = [ring(0, p, d, 1, own(0)) for d in (0, 1)]
    y = [across(k, 0, 4, own(1))]
    fill(0)
    ya.wait_recv()
    a1 = [ring(0, q, d, 1) for d in (0, 1)]
    for s in range(2, m + 1):
        nb, n0, n1 = [], [], []
        for d in (0, 1):
            b[d].wait_recv()
            nb.append(ring(1, p, d, s))
            y.append(across(origin(d, s - 1), 0, 4))
        for d in (0, 1):
            a0[d].wait_recv()
            n0.append(ring(0, p, d, s))
        fill(s - 1)
        for d in (0, 1):
            a1[d].wait_recv()
            n1.append(ring(0, q, d, s))
        b, a0, a1 = nb, n0, n1
    fill(m)
    for d in (0, 1):
        b[d].wait_recv()
        y.append(across(origin(d, m), 2 * d, 2))

    def done_a():
        for c in a0 + a1:
            c.wait_recv()

    def done_b():
        for c in y:
            c.wait_recv()

    return done_a, done_b


def scatter(net, n, k, p, dev, part, bufs, out, fill):
    m = n // 2
    sa, ra, sb, rb, sy, ry, sya, rya = bufs
    q = 1 - p
    both = (0, 1)

    def side(d):
        return dev(wrap(k + 1, n) if d == 0 else wrap(k - 1, n), p)

    def emit(dst, lo, cnt, terms):
        def one(i, unused):
            total = terms[0](i)
            for t in terms[1:]:
                total = total + t(i)
            dst[i] = total.astype(BF)
            return unused

        lax.fori_loop(lo, lo + cnt, one, 0)

    def read(ref):
        return lambda i: ref[i].astype(F32)

    def mine(g, pp, t):
        return lambda i: part(g, pp, t, i)

    def send_y(o):
        emit(sy.at[o], 0, 4, [mine(1, q, wrap(k + o, n))])
        return net.copy(sy.at[o], ry.at[o], dev(k, q))

    def step(src, dst, d, s, terms, before):
        if s == 1:
            lo, cnt = 2 * d, 2
            emit(src, lo, cnt, terms)
            return net.copy(src.at[pl.ds(lo, cnt)], dst.at[pl.ds(lo, cnt)], side(d))
        if s == 2:
            emit(src, 2 * d, 2, terms + [read(before)])
            emit(src, 2 - 2 * d, 2, terms)
        else:
            emit(src, 0, 4, terms + [read(before)])
        return net.copy(src, dst, side(d))

    def offset(d, s):
        return m + 1 - s if d == 0 else (n - (m + 1 - s)) % n

    ys = {m: send_y(m)}
    a, b = {}, {}
    for s in range(1, m + 1):
        for j, pp in ((0, q), (1, p)):
            for d in both:
                if s > 1:
                    a[j, d].wait_recv()
                t = wrap(k + offset(d, s), n)
                a[j, d] = step(
                    sa.at[j, d, s - 1], ra.at[j, d, s - 1], d, s, [mine(0, pp, t)], ra.at[j, d, max(s - 2, 0)]
                )
            if s == 1 and j == 0:
                for e in both:
                    o = offset(e, 2)
                    if o not in ys:
                        ys[o] = send_y(o)
        if s == 1:
            for e in range(3, m + 1):
                for d in both:
                    ys[offset(d, e)] = send_y(offset(d, e))
            ys[0] = send_y(0)
        for d in both:
            o = offset(d, s)
            if not (s == 1 and d == 1):
                ys[o].wait_recv()
            if s > 1:
                b[d].wait_recv()
            t = wrap(k + o, n)
            b[d] = step(
                sb.at[d, s - 1],
                rb.at[d, s - 1],
                d,
                s,
                [mine(1, p, t), read(ry.at[o])],
                rb.at[d, max(s - 2, 0)],
            )
        fill(s)
    for d in both:
        a[0, d].wait_recv()
    emit(sya, 0, 4, [mine(0, q, k), read(ra.at[0, 0, m - 1]), read(ra.at[0, 1, m - 1])])
    ya = net.copy(sya, rya, dev(k, q))
    ys[0].wait_recv()
    for d in both:
        b[d].wait_recv()
    emit(out.at[1], 0, 4, [mine(1, p, k), read(ry.at[0]), read(rb.at[0, m - 1]), read(rb.at[1, m - 1])])
    for d in both:
        a[1, d].wait_recv()
    ya.wait_recv()
    emit(
        out.at[0],
        0,
        4,
        [mine(0, p, k), read(ra.at[1, 0, m - 1]), read(ra.at[1, 1, m - 1]), read(rya)],
    )


def kernel(
    x_ref, w_ref, cot_ref, tiles_ref, idx_ref, act_ref, fg_ref, wg_ref,
    tiles, flipped, idx, xs, g0, g1, sums, aggs, af, dself, dother, dg, fgs, fo,
    fa_s, fa_r, fb_s, fb_r, fy_s, fy_r, fya_s, fya_r,
    ba_s, ba_r, bb_s, bb_r, by_s, by_r, bya_s, bya_r,
    wpart, wpair, wrow, wmine, wcol, wfull,
    local, send, recv,
):
    row, col = lax.axis_index("row"), lax.axis_index("col")
    p, z = lax.div(row, NZ), lax.rem(row, NZ)
    h = lax.rem(col, 2)
    chip = lax.div(col, 2)
    x, u = lax.div(chip, 2), lax.rem(chip, 2)
    other = (row, col + 1 - 2 * h)
    net = Net(send, recv)

    def row_dev(k, pp):
        return (pp * NZ + k, col)

    def col_dev(k, pp):
        return (row, (k * 2 + pp) * 2 + h)

    mates = [(wrap(row + d, 16), col) for d in range(1, 16)]
    chips = [(row, wrap(chip + d, 8) * 2 + h) for d in range(1, 8)]

    barrier = pltpu.get_barrier_semaphore()
    for device in mates + chips + [other]:
        pl.semaphore_signal(barrier, inc=1, device_id=device, device_id_type=MESH)

    mine = pl.ds(pl.multiple_of(h * TB, TB), TB)
    theirs = pl.ds(pl.multiple_of((1 - h) * TB, TB), TB)
    cx = pltpu.make_async_copy(x_ref.at[:, :, mine], xs.at[h], local.at[0])
    ct = pltpu.make_async_copy(tiles_ref, tiles.at[h], local.at[1])
    ci = pltpu.make_async_copy(idx_ref, idx.at[h], local.at[2])
    for c in (cx, ct, ci):
        c.start()
    sums[0] = jnp.zeros((TB, TB), F32)
    sums[SLOTS] = jnp.zeros((TB, TB), F32)
    pl.semaphore_wait(barrier, 23)

    rx = net.copy(x_ref.at[:, :, theirs], xs.at[h], other)
    ri = net.copy(idx_ref, idx.at[h], other)
    rt = net.copy(tiles_ref, tiles.at[h], other)
    cx.wait()
    rx.wait_recv()

    gs = (g0, g1)

    def g_slot(g, pp, k, lo, cnt):
        return gs[g].at[pl.ds((pp * NZ + k) * 4 + lo, cnt)]

    def flip(lo, cnt):
        def one(t, unused):
            for g in (0, 1):
                flipped[g, t] = tiles[g, t].T
            return unused

        lax.fori_loop(lo, lo + cnt, one, 0)

    def fill_first(s):
        if s == 0:
            for g in (0, 1):
                gs[g][pl.ds(row * 4, 4)] = xs[g]
        if s == 1:
            ct.wait()
            ci.wait()
            rt.wait_recv()
            ri.wait_recv()
        if s >= 1:
            flip((s - 1) * 8, 8)

    done_a, done_b = gather(net, NZ, z, p, row_dev, lambda g: xs.at[g], g_slot, fill_first)

    def multiply(g, blocks, source, at):
        def one(t, unused):
            block = blocks[g, idx[g, at, t]]
            product = dot(block, source[idx[g, at + 1, t]], 1, 0)
            keep = idx[g, at + 2, t].astype(F32)
            sums[g * SLOTS + 1 + t] = product + keep * sums[g * SLOTS + t]
            return unused

        lax.fori_loop(0, NT, one, 0, unroll=4)

    done_a()
    multiply(0, tiles, g0, 0)
    done_b()
    multiply(1, tiles, g1, 0)

    def forward_part(g, pp, k, i):
        at = ((k * 2 + pp) * 2 + g) * 4 + i
        return sums[idx[0, 3, at]] + sums[SLOTS + idx[1, 3, at]]

    scatter(
        net, NX, x, u, col_dev, forward_part,
        (fa_s, fa_r, fb_s, fb_r, fy_s, fy_r, fya_s, fya_r), aggs, lambda s: None,
    )
    ra = net.copy(aggs.at[1 - h], af.at[h], other)
    af[h] = aggs[h]
    ra.wait_recv()

    agg = jnp.concatenate([af[0].reshape(512, TB), af[1].reshape(512, TB)], axis=1)
    pre = dot(agg, w_ref[...], 1, 0)
    sigma = jax.nn.sigmoid(pre)
    act_ref[...] = (pre * sigma).astype(BF)
    dpre = (cot_ref[...].astype(F32) * sigma * (1.0 + pre * (1.0 - sigma))).astype(BF)
    dagg = dot(dpre, w_ref[...], 1, 1).astype(BF)
    halves = (dagg[:, :TB].reshape(4, TB, TB), dagg[:, TB:].reshape(4, TB, TB))
    dother[0] = halves[0]
    dother[1] = halves[1]
    rd = net.copy(dother.at[1 - h], dself.at[h], other)
    dself[h] = dother[h]
    wpart[...] = dot(agg, dpre, 0, 0)
    rd.wait_recv()

    def d_slot(g, pp, k, lo, cnt):
        return dg.at[pl.ds(((k * 2 + pp) * 2 + g) * 4 + lo, cnt)]

    weights = {}

    def fill_second(s):
        if s == 0:
            weights[0] = net.copy(
                wpart.at[pl.ds(pl.multiple_of((1 - h) * TB, TB), TB)], wpair, other
            )
            dg[pl.ds(chip * 8, 4)] = dself[0]
            dg[pl.ds(chip * 8 + 4, 4)] = dself[1]
        if s == 1:
            weights[0].wait_recv()
            wpair[...] = wpair[...] + wpart[pl.ds(pl.multiple_of(h * TB, TB), TB)]
        if s == 2:
            weights[1] = [
                net.copy(wpair.at[pl.ds(pl.multiple_of(d[0] * 8, 8), 8)], wrow.at[row], d) for d in mates
            ]
            wrow[row] = wpair[pl.ds(pl.multiple_of(row * 8, 8), 8)]

    done_a, done_b = gather(net, NX, x, u, col_dev, lambda g: dself.at[g], d_slot, fill_second)
    done_a()
    done_b()
    multiply(0, flipped, dg, 4)
    multiply(1, flipped, dg, 4)

    def backward_part(g, pp, k, i):
        return sums[g * SLOTS + idx[g, 7, (pp * NZ + k) * 4 + i]]

    def fill_third(s):
        if s == 1:
            for c in weights[1]:
                c.wait_recv()
            total = wrow[0]
            for i in range(1, 16):
                total = total + wrow[i]
            wmine[...] = total
            wcol[chip] = total
            weights[2] = [net.copy(wmine, wcol.at[chip], d) for d in chips]
        if s == 2:
            for c in weights[2]:
                c.wait_recv()
            total = wcol[0]
            for i in range(1, 8):
                total = total + wcol[i]
            here = pl.ds(pl.multiple_of(h * TB + row * 8, 8), 8)
            wfull[here] = total
            weights[3] = [net.copy(wfull.at[here], wfull.at[here], d) for d in mates]
        if s == 3:
            for c in weights[3]:
                c.wait_recv()
            half = pl.ds(pl.multiple_of(h * TB, TB), TB)
            weights[4] = net.copy(wfull.at[half], wfull.at[half], other)
        if s == 4:
            weights[4].wait_recv()
            wg_ref[...] = wfull[...]

    scatter(
        net, NZ, z, p, row_dev, backward_part,
        (ba_s, ba_r, bb_s, bb_r, by_s, by_r, bya_s, bya_r), fgs, fill_third,
    )
    rf = net.copy(fgs.at[1 - h], fo.at[h], other)
    fo[h] = fgs[h]
    rf.wait_recv()
    fg_ref[:, :TB] = fo[0].reshape(512, TB)
    fg_ref[:, TB:] = fo[1].reshape(512, TB)
    net.finish()


def order_of(targets, sources):
    key = targets * 64 + sources
    rank = jnp.sum((key[None, :] < key[:, None]).astype(jnp.int32), axis=1)
    place = (rank[None, :] == jnp.arange(NT)[:, None]).astype(jnp.int32)
    before = (rank[None, :] == jnp.arange(NT)[:, None] - 1).astype(jnp.int32)
    perm = jnp.sum(place * jnp.arange(NT)[None, :], axis=1)
    source = jnp.sum(place * sources[None, :], axis=1)
    now = jnp.sum(place * targets[None, :], axis=1)
    last = jnp.sum(before * (targets + 1)[None, :], axis=1) - 1
    same = (now == last).astype(jnp.int32)
    blocks = jnp.arange(64)
    upto = jnp.sum((targets[None, :] <= blocks[:, None]).astype(jnp.int32), axis=1)
    found = jnp.max((targets[None, :] == blocks[:, None]).astype(jnp.int32), axis=1)
    wide = lambda v: jnp.pad(v, (0, 128 - v.shape[0]))
    return [wide(perm), wide(source), wide(same), wide(upto * found)]


def body(features, weight, cotangent, tiles, coords):
    rows, cols = coords[0, 0, 0], coords[0, 0, 1]
    idx = jnp.stack(order_of(rows, cols) + order_of(cols, rows)).astype(jnp.int32)
    vmem = pl.BlockSpec(memory_space=pltpu.VMEM)
    hbm = pl.BlockSpec(memory_space=pl.ANY)
    unit = (4, TB, TB)

    def sums_for(n):
        m = n // 2
        return [
            pltpu.VMEM((*s, *unit), BF)
            for s in ((2, 2, m), (2, 2, m), (2, m), (2, m), (n,), (n,), (), ())
        ]

    act, fg, wg = pl.pallas_call(
        kernel,
        out_shape=(
            jax.ShapeDtypeStruct((512, 256), BF),
            jax.ShapeDtypeStruct((512, 256), BF),
            jax.ShapeDtypeStruct((256, 256), F32),
        ),
        in_specs=[hbm, vmem, vmem, hbm, hbm],
        out_specs=(vmem, vmem, vmem),
        scratch_shapes=[
            pltpu.VMEM((2, NT, TB, TB), BF),
            pltpu.VMEM((2, NT, TB, TB), BF),
            pltpu.SMEM((2, 8, 128), jnp.int32),
            pltpu.VMEM((2, *unit), BF),
            pltpu.VMEM((64, TB, TB), BF),
            pltpu.VMEM((64, TB, TB), BF),
            pltpu.VMEM((2 * SLOTS, TB, TB), F32),
            pltpu.VMEM((2, *unit), BF),
            pltpu.VMEM((2, *unit), BF),
            pltpu.VMEM((2, *unit), BF),
            pltpu.VMEM((2, *unit), BF),
            pltpu.VMEM((64, TB, TB), BF),
            pltpu.VMEM((2, *unit), BF),
            pltpu.VMEM((2, *unit), BF),
            *sums_for(NX),
            *sums_for(NZ),
            pltpu.VMEM((256, 256), F32),
            pltpu.VMEM((128, 256), F32),
            pltpu.VMEM((16, 8, 256), F32),
            pltpu.VMEM((8, 256), F32),
            pltpu.VMEM((8, 8, 256), F32),
            pltpu.VMEM((256, 256), F32),
            pltpu.SemaphoreType.DMA((3,)),
            pltpu.SemaphoreType.DMA((SEMS,)),
            pltpu.SemaphoreType.DMA((SEMS,)),
        ],
        compiler_params=pltpu.CompilerParams(
            collective_id=0, has_side_effects=True, vmem_limit_bytes=56 * 2**20
        ),
        cost_estimate=pl.CostEstimate(flops=10**9, bytes_accessed=4 * 2**20, transcendentals=2**17),
        name="layer",
    )(features.reshape(4, TB, 256), weight, cotangent, tiles.reshape(NT, TB, TB), idx)
    return act, fg, wg


def solution(mesh):
    return jax.shard_map(
        body,
        mesh=mesh,
        in_specs=(
            P(("col", "row"), None),
            P(),
            P(("row", "col"), None),
            P("row", "col", None, None, None),
            P("row", "col", None, None),
        ),
        out_specs=(P(("row", "col"), None), P(("col", "row"), None), P()),
        check_vma=False,
    )
```

time: 675 us -> 145 us (0.21)
  waiting for transfers between devices: 599 us -> 0 us
  Pallas kernels: 0 us -> 139 us
  local copies, waits for them, and re-layouts: 28.1 us -> 4.76 us
  other arithmetic: 22.5 us -> 0.58 us
  between operations: 13.8 us -> 0.76 us
  matrix products: 9.48 us -> 0 us
    psum x1 -> x0, waiting for transfers between devices: 251 us -> none  [body(): weight_grad = lax.psum(partial_weight, ('row', 'col'))]
    reduce_scatter x2 -> x0, waiting for transfers between devices: 213 us -> none  [the longest x1 115 us: body(): lax.psum_scatter(forward, 'col', scatter_dimension=0, tiled=True)]
    pallas_call x0 -> x1, Pallas kernels: none -> 139 us  [body(): pl.pallas_call(kernel, out_shape=(jax.ShapeDtypeStruct((512, 256), BF), j...]
    all_gather x2 -> x0, waiting for transfers between devices: 135 us -> none  [the longest x1 73 us: body(): lax.all_gather(features, 'row', axis=0, tiled=True)]
    scatter-add x2 -> x0, other arithmetic: 20 us -> none  [advance(): return (carry.at[target_now].add(products), None)]
    dot_general x2 -> x0, local copies, waits for them, and re-layouts: 11.2 us -> none  [the longest x1 5.62 us: advance(): jnp.einsum('gab,gbf->gaf', blocks_now, picked, preferred_element_type=jnp...]
    dot_general x5 -> x0, matrix products: 9.48 us -> none  [the longest x1 2.7 us: advance(): jnp.einsum('gab,gbf->gaf', blocks_now, picked, preferred_element_type=jnp...]
    another operation x2 -> x7, local copies, waits for them, and re-layouts: 8.51 us -> 0.64 us  [body(): jnp.stack(order_of(rows, cols) + order_of(cols, rows)).astype(jnp.int32)]
  transfers between devices with their start and end apart: 5 -> 0, of which waited for: 5 -> 0; matrix products, arithmetic and copies ran while one was open for 1% -> 0% of each run, Pallas kernels for 0% -> 0%
where the time goes in v1:
time: 145 us
  Pallas kernels  139 us (96%)
  local copies, waits for them, and re-layouts  4.76 us (3%)
    pallas_call x1, Pallas kernels, body(): pl.pallas_call(kernel, out_shape=(jax.ShapeDtypeStruct((512, 256), BF), j...  139 us
    unnamed x9, local copies, waits for them, and re-layouts  4.12 us

profile of v1, /device:TPU:1, one launch (start us, length us, event | category | flops | bytes accessed | tf_op | source)
XLA Modules:
  0.0 144.7 jit_solution(16926615066536142235)
XLA Ops:
  0.6 0.0 copy-start.2
  0.7 0.7 copy-done.2
  1.3 0.1 convert_reduce_fusion
  1.5 0.2 convert_reduce_fusion.2
  1.7 0.3 select_reduce_fusion
  2.0 0.6 stack.43.idx_ref
  2.6 138.6 %layer.1 = (bf16[512,256]{1,0:T(8,128)(2,1)}, bf16[512,256]{1,0:T(8,128)(2,1)}, f32[256,256]{1,0:T(8,128)}) custom-call(bf16[4,128,256]{2,1,0:T(8,128)(2,1)} %bitcast.35, bf16[256,256]{1,0:T(8,128)(2,1)} %w_ref.1, bf16[512,256]{1,0:T(8,128)(2,1)} %cot_ref.1, bf16[32,128,128]{2,1,0:T(8,128)(2,1)} %bitcast.34, s32[8,128]{1,0:T(8,128)} %stack.43.idx_ref), custom_call_target="tpu_custom_call" | custom-call | flops 1000000000 | bytes 4194304 | tf_op jit(solution)/shard_map/layer/pallas_call | solution.py:422
  141.3 0.0 copy-start.1
  141.3 1.7 %copy.11 = bf16[512,256]{1,0:T(8,128)(2,1)} copy(bf16[512,256]{1,0:T(8,128)(2,1)} %get-tuple-element.28) | data formatting | bytes 524288
  143.0 0.0 copy-done.1
  143.0 0.0 copy-start
  143.0 0.7 copy.12
  143.7 0.3 copy-done
  144.0 0.7 copy.13
  (15 shorter events, 0.1 us)
Async XLA Ops:
  0.6 0.7 copy-start.2
  141.3 1.7 %copy-start.1 = (bf16[512,256]{1,0:T(8,128)(2,1)S(1)}, bf16[512,256]{1,0:T(8,128)(2,1)}, u32[]{:S(2)}) copy-start(bf16[512,256]{1,0:T(8,128)(2,1)} %get-tuple-element.29) | copy-start | bytes 786436
  143.0 1.0 copy-start

commit v2 on v0

v2 whole, which is shorter than its diff:
```python
import jax
import jax.numpy as jnp
from jax import lax
from jax.experimental import pallas as pl
from jax.experimental.pallas import tpu as pltpu
from jax.sharding import PartitionSpec as P

MESH = pl.DeviceIdType.MESH
BF = jnp.bfloat16
F32 = jnp.float32
TB = 128
NT = 32
NZ = 8
NX = 4
SLOTS = NT + 1
SIZES = (64, 64)
PLAN_X = ('ab', 'ba')
PLAN_F = ('aa', 'ab')
PLAN_D = ('ba', 'aa')
PLAN_B = ('ab', 'ba')
GATE_X = 2
GATE_D = 2
RANKS = ((0, 0), (0, 0))
SEMS = 320
INF = 1e9


def dot(a, b, da, db):
    return lax.dot_general(a, b, (((da,), (db,)), ((), ())), preferred_element_type=F32)


def wrap(v, n):
    return lax.rem(v + n, n)


class Handle:
    def __init__(self, copy, left, eta):
        self.copy, self.left, self.eta = copy, left, eta
        self.waited = self.sent = False

    def wait(self):
        if not self.waited:
            self.copy.wait_recv()
            self.waited = True

    def wait_send(self):
        if not self.sent:
            self.copy.wait_send()
            self.sent = True


class Count:
    def __init__(self, net, need):
        self.net, self.need, self.eta = net, need, INF

    def hit(self):
        self.need -= 1
        if self.need == 0:
            self.eta = self.net.now

    def wait(self):
        pass


class Later:
    def __init__(self):
        self.handle = None

    @property
    def eta(self):
        return INF if self.handle is None else self.handle.eta

    def wait(self):
        self.handle.wait()


class Net:
    def __init__(self, send, recv):
        self.send, self.recv, self.used, self.started = send, recv, 0, []
        self.now, self.free, self.tasks, self.turn, self.fillers = 0.0, {}, [], 0, []

    def copy(self, src, dst, device, link, size):
        c = pltpu.make_async_remote_copy(
            src_ref=src,
            dst_ref=dst,
            send_sem=self.send.at[self.used],
            recv_sem=self.recv.at[self.used],
            device_id=device,
            device_id_type=MESH,
        )
        self.used += 1
        c.start()
        rate = 400.0 if link == "c" else 43.0
        late = {"c": 1.0, "y2": 2.7, "x2": 2.7, "w": 8.0}.get(link, 1.6)
        names = {"y2": ("y",), "x2": ("x+", "x-")}.get(link, (link,))
        start = max([self.now] + [self.free.get(name, 0.0) for name in names])
        left = start + size / 1000.0 / rate
        for name in names:
            self.free[name] = left
        self.now += 0.08
        handle = Handle(c, left, left + late)
        self.started.append(handle)
        return handle

    def spawn(self, task, rank=0):
        self.turn += 1
        self.tasks.append([task, None, rank, self.turn])

    def run(self):
        while self.tasks:
            best, key = None, None
            for t in self.tasks:
                eta = self.now if t[1] is None else max(t[1].eta, self.now)
                k = (eta, t[2], t[3])
                if key is None or k < key:
                    best, key = t, k
            assert key[0] < INF, "stuck"
            if key[0] - self.now > 0.6 and self.fillers:
                cost, work = self.fillers.pop(0)
                work()
                self.now += cost
                continue
            old = [e for e in self.started if not e.sent and e.left + 4.0 < self.now]
            for e in old[: max(0, int((key[0] - self.now) / 0.04))]:
                e.wait_send()
                self.now += 0.03
            self.now = max(self.now, key[0])
            if best[1] is not None:
                best[1].wait()
            self.turn += 1
            best[3] = self.turn
            try:
                best[1] = next(best[0])
            except StopIteration:
                self.tasks.remove(best)
        for cost, work in self.fillers:
            work()
        self.fillers = []

    def finish(self):
        for e in self.started:
            e.wait_send()


class Ring:
    def __init__(self, net, n, k, p, dev, axis, y, fc):
        self.net, self.n, self.m, self.k, self.p, self.q = net, n, n // 2, k, p, 1 - p
        self.dev, self.axis, self.y, self.fc = dev, axis, y, fc

    def side(self, d):
        return self.dev(wrap(self.k + 1, self.n) if d == 0 else wrap(self.k - 1, self.n), self.p)

    def ring(self, src, dst, d, cnt):
        return self.net.copy(src, dst, self.side(d), self.axis + "+-"[d], cnt * self.fc * TB * 2)

    def place(self, o):
        return (None, "x+", "x2", "x-")[o], self.dev(wrap(self.k + o, self.n), self.p)

    def straight(self, src, dst, o, cnt):
        link, device = self.place(o)
        return self.net.copy(src, dst, device, link, cnt * self.fc * TB * 2)

    def across(self, src, dst, cnt):
        return self.net.copy(src, dst, self.dev(self.k, self.q), self.y, cnt * self.fc * TB * 2)

    def gather(self, plan, own, slot, rank, gate):
        net, m, n, k, p, q = self.net, self.m, self.n, self.k, self.p, self.q
        if plan in "de":
            return self.gather_straight(plan, own, slot, rank)
        first = plan == "a"
        issued = Count(net, 4 if first else 2)
        done = Count(net, 4 if first else 2 * m + 3)

        def origin(d, s):
            return wrap(k - s, n) if d == 0 else wrap(k + s, n)

        def arrive(c):
            yield c
            done.hit()

        def over(o, lo, cnt, src):
            net.spawn(arrive(self.across(src, slot(p, o, lo, cnt), cnt)), rank)

        def chain(pp, d, src, c):
            if c is not None:
                yield c
            for s in range(1, m + 1):
                o = origin(d, s - 1)
                lo, cnt = (0, 4) if s < m else (2 * d, 2)
                here = slot(pp, o, lo, cnt) if s > 1 or src is None else src
                c = self.ring(here, slot(pp, o, lo, cnt), d, cnt)
                if s > 1 and not first:
                    over(o, 0, 4, slot(pp, o, 0, 4))
                if s == gate:
                    issued.hit()
                if s < m:
                    yield c
            yield c
            if not first:
                o = origin(d, m)
                over(o, 2 * d, 2, slot(pp, o, 2 * d, 2))
            done.hit()

        if first:
            ya = self.across(own, slot(p, k, 0, 4), 4)
            for d in (0, 1):
                net.spawn(chain(p, d, own, None), rank)
            for d in (0, 1):
                net.spawn(chain(q, d, None, ya), rank)
        else:
            for d in (0, 1):
                net.spawn(chain(p, d, own, None), rank)

            def start():
                yield None
                over(k, 0, 4, own)

            net.spawn(start(), rank)
        return issued, done

    def gather_straight(self, plan, own, slot, rank):
        net, n, k, p, q = self.net, self.n, self.k, self.p, self.q
        offsets = (2, 1, 3)
        issued = Count(net, 1)
        done = Count(net, 6 if plan == "e" else 4)

        def arrive(c):
            yield c
            done.hit()

        if plan == "e":
            ya = self.across(own, slot(p, k, 0, 4), 4)
            for o in offsets:
                net.spawn(arrive(self.straight(own, slot(p, k, 0, 4), o, 4)), rank)

            def onward():
                yield ya
                for o in offsets:
                    net.spawn(arrive(self.straight(slot(q, k, 0, 4), slot(q, k, 0, 4), o, 4)), rank)
                issued.hit()

            net.spawn(onward(), rank)
        else:
            net.spawn(arrive(self.across(own, slot(p, k, 0, 4), 4)), rank)
            came = {o: self.straight(own, slot(p, k, 0, 4), o, 4) for o in offsets}
            issued.hit()

            def onward(o):
                yield came[o]
                t = slot(p, wrap(k - o, n), 0, 4)
                net.spawn(arrive(self.across(t, t, 4)), rank)

            for o in offsets:
                net.spawn(onward(o), rank)
        return issued, done

    def scatter(self, plan, part, bufs, out, rank):
        net, m, n, k, p, q = self.net, self.m, self.n, self.k, self.p, self.q
        done = Count(net, 1)

        def emit(dst, lo, cnt, terms):
            def one(i, unused):
                total = terms[0](i)
                for t in terms[1:]:
                    total = total + t(i)
                dst[i] = total.astype(BF)
                return unused

            lax.fori_loop(lo, lo + cnt, one, 0)
            net.now += 0.05 * cnt

        def read(ref):
            return lambda i: ref[i].astype(F32)

        def mine(pp, t):
            return lambda i: part(pp, t, i)

        def offset(d, s):
            return m + 1 - s if d == 0 else (n - (m + 1 - s)) % n

        def step(src, dst, d, s, terms, before):
            if s == 1:
                lo = 2 * d
                emit(src, lo, 2, terms)
                return self.ring(src.at[pl.ds(lo, 2)], dst.at[pl.ds(lo, 2)], d, 2)
            if s == 2:
                emit(src, 2 * d, 2, terms + [read(before)])
                emit(src, 2 - 2 * d, 2, terms)
            else:
                emit(src, 0, 4, terms + [read(before)])
            return self.ring(src, dst, d, 4)

        if plan in "de":
            offsets = (2, 1, 3)
        if plan == "e":
            sa, ra, sya, rya = bufs

            def final():
                came = {}
                for j, pp in ((0, q), (1, p)):
                    for o in offsets:
                        emit(sa.at[j, o], 0, 4, [mine(pp, wrap(k + o, n))])
                        came[j, o] = self.straight(sa.at[j, o], ra.at[j, o], o, 4)
                        yield None
                for o in offsets:
                    yield came[0, o]
                emit(sya, 0, 4, [mine(q, k)] + [read(ra.at[0, o]) for o in offsets])
                c = self.across(sya, rya, 4)
                for o in offsets:
                    yield came[1, o]
                yield c
                emit(out, 0, 4, [mine(p, k)] + [read(ra.at[1, o]) for o in offsets] + [read(rya)])
                done.hit()

            net.spawn(final(), rank)
        elif plan == "d":
            sb, rb, sy, ry = bufs

            def final():
                ys, came = {}, {}
                for o in offsets + (0,):
                    emit(sy.at[o], 0, 4, [mine(q, wrap(k + o, n))])
                    ys[o] = self.across(sy.at[o], ry.at[o], 4)
                    yield None
                for o in offsets:
                    yield ys[o]
                    emit(sb.at[o], 0, 4, [mine(p, wrap(k + o, n)), read(ry.at[o])])
                    came[o] = self.straight(sb.at[o], rb.at[o], o, 4)
                yield ys[0]
                for o in offsets:
                    yield came[o]
                emit(out, 0, 4, [mine(p, k), read(ry.at[0])] + [read(rb.at[o]) for o in offsets])
                done.hit()

            net.spawn(final(), rank)
        elif plan == "a":
            sa, ra, sya, rya = bufs
            rings = [Count(net, 2), Count(net, 2)]

            def chain(j, pp, d):
                for s in range(1, m + 1):
                    t = wrap(k + offset(d, s), n)
                    c = step(sa.at[j, d, s - 1], ra.at[j, d, s - 1], d, s, [mine(pp, t)], ra.at[j, d, max(s - 2, 0)])
                    yield c
                rings[j].hit()

            def last(j):
                return [read(ra.at[j, 0, m - 1]), read(ra.at[j, 1, m - 1])]

            def final():
                yield rings[0]
                emit(sya, 0, 4, [mine(q, k)] + last(0))
                c = self.across(sya, rya, 4)
                yield rings[1]
                yield c
                emit(out, 0, 4, [mine(p, k)] + last(1) + [read(rya)])
                done.hit()

            for j, pp in ((0, q), (1, p)):
                for d in (0, 1):
                    net.spawn(chain(j, pp, d), rank)
            net.spawn(final(), rank)
        else:
            sb, rb, sy, ry = bufs
            ys = [Later() for i in range(n)]
            rings = Count(net, 2)

            def send():
                order = [m]
                for s in range(2, m + 1):
                    order += [offset(0, s), offset(1, s)]
                for o in order + [0]:
                    emit(sy.at[o], 0, 4, [mine(q, wrap(k + o, n))])
                    ys[o].handle = self.across(sy.at[o], ry.at[o], 4)
                    yield None

            def chain(d):
                for s in range(1, m + 1):
                    o = offset(d, s)
                    yield ys[o]
                    terms = [mine(p, wrap(k + o, n)), read(ry.at[o])]
                    c = step(sb.at[d, s - 1], rb.at[d, s - 1], d, s, terms, rb.at[d, max(s - 2, 0)])
                    yield c
                rings.hit()

            def final():
                yield rings
                yield ys[0]
                emit(out, 0, 4, [mine(p, k), read(ry.at[0]), read(rb.at[0, m - 1]), read(rb.at[1, m - 1])])
                done.hit()

            net.spawn(send(), rank)
            for d in (0, 1):
                net.spawn(chain(d), rank)
            net.spawn(final(), rank)
        return done


def kernel(
    x_hbm, w_hbm, cot_hbm, tiles_hbm, idx_hbm, act_ref, fg_ref, wg_ref,
    xv, wv, cotv, wt, cott, tiles, idx, xo, xs, gs, sums, aggs, af, dall, ds, dg, fgs, fo,
    fbufs, bbufs, wpart, wpair, wrow, wmine, wcol, wfull,
    local, send, recv,
):
    row, col = lax.axis_index("row"), lax.axis_index("col")
    p, z = lax.div(row, NZ), lax.rem(row, NZ)
    h = lax.rem(col, 2)
    chip = lax.div(col, 2)
    x, u = lax.div(chip, 2), lax.rem(chip, 2)
    other = (row, col + 1 - 2 * h)
    net = Net(send, recv)
    along_z = [Ring(net, NZ, z, p, lambda k, pp: (pp * NZ + k, col), "z", "y", fc) for fc in SIZES]
    along_x = [Ring(net, NX, x, u, lambda k, pp: (row, (k * 2 + pp) * 2 + h), "x", "y2", fc) for fc in SIZES]
    mates = [(wrap(row + d, 16), col) for d in range(1, 16)]
    chips = [(row, wrap(chip + d, 8) * 2 + h) for d in range(1, 8)]
    chunks = range(len(SIZES))
    offsets = [sum(SIZES[:c]) for c in chunks]
    bytes_of = [4 * fc * TB * 2 for fc in SIZES]

    barrier = pltpu.get_barrier_semaphore()
    for device in mates + chips + [other]:
        pl.semaphore_signal(barrier, inc=1, device_id=device, device_id_type=MESH)

    pairs = ((x_hbm, xv), (idx_hbm, idx.at[h]), (tiles_hbm, tiles.at[h]), (w_hbm, wv), (cot_hbm, cotv))
    loads = [pltpu.make_async_copy(a, b, local.at[i]) for i, (a, b) in enumerate(pairs)]
    for c in loads:
        c.start()
    for c in chunks:
        sums[c][0] = jnp.zeros((SIZES[c], TB), F32)
        sums[c][SLOTS] = jnp.zeros((SIZES[c], TB), F32)

    mine = pl.ds(pl.multiple_of(h * TB, TB), TB)
    theirs = pl.ds(pl.multiple_of((1 - h) * TB, TB), TB)
    loads[0].wait()
    for b in range(4):
        block = xv[b, :, theirs].T
        for c in chunks:
            xo[c][b] = block[offsets[c]:offsets[c] + SIZES[c]]
    for b in range(4):
        block = xv[b, :, mine].T
        for c in chunks:
            xs[c][h, b] = block[offsets[c]:offsets[c] + SIZES[c]]
    pl.semaphore_wait(barrier, 23)

    rx = [net.copy(xo[c], xs[c].at[h], other, "c", bytes_of[c]) for c in chunks]
    ri = net.copy(idx_hbm, idx.at[h], other, "c", 4096)
    rt = net.copy(tiles_hbm, tiles.at[h], other, "c", 2**20)

    def g_slot(c, g):
        return lambda pp, k, lo, cnt: gs[c][g].at[pl.ds((pp * NZ + k) * 4 + lo, cnt)]

    def d_slot(c, g):
        return lambda pp, k, lo, cnt: dg[c].at[pl.ds(((k * 2 + pp) * 2 + g) * 4 + lo, cnt)]

    def multiply(c, g, source, at, side):
        def one(t, unused):
            product = dot(source[idx[g, at + 1, t]], tiles[g, idx[g, at, t]], 1, side)
            keep = idx[g, at + 2, t].astype(F32)
            sums[c][g * SLOTS + 1 + t] = product + keep * sums[c][g * SLOTS + t]
            return unused

        lax.fori_loop(0, NT, one, 0, unroll=4)
        net.now += 0.35

    def forward_part(c, g):
        def part(pp, k, i):
            at = ((k * 2 + pp) * 2 + g) * 4 + i
            return sums[c][idx[0, 3, at]] + sums[c][SLOTS + idx[1, 3, at]]

        return part

    def backward_part(c, g):
        return lambda pp, k, i: sums[c][g * SLOTS + idx[g, 7, (pp * NZ + k) * 4 + i]]

    issued_x = [None] * len(SIZES)

    def forward(c):
        if c:
            for e in issued_x[c - 1]:
                yield e
        rx[c].wait()
        events = [along_z[c].gather(PLAN_X[c][g], xs[c].at[g], g_slot(c, g), RANKS[0][0] + c, GATE_X) for g in (0, 1)]
        issued_x[c] = [e[0] for e in events]
        for g in (0, 1):
            gs[c][g][pl.ds(row * 4, 4)] = xs[c][g]
        if c + 1 < len(SIZES):
            net.spawn(forward(c + 1), RANKS[0][0] + c + 1)
        if c == 0:
            for e in loads[1:3]:
                e.wait()
            yield ri
            yield rt
        for g in (0, 1):
            yield events[g][1]
            multiply(c, g, gs[c][g], 0, 1)
        dones = [
            along_x[c].scatter(PLAN_F[c][g], forward_part(c, g), fbufs[c][g], aggs[c].at[g], RANKS[0][1] + c)
            for g in (0, 1)
        ]
        for e in dones:
            yield e
        ra = net.copy(aggs[c].at[1 - h], af[c].at[h], other, "c", bytes_of[c])
        af[c][h] = aggs[c][h]
        yield ra

    def turn_weight():
        loads[3].wait()
        wt[...] = wv[...].T

    def turn_cotangent(i):
        def work():
            if i == 0:
                loads[4].wait()
            here = slice(i * TB, (i + 1) * TB)
            cott[:, here] = cotv[here, :].T

        return work

    net.fillers = [(0.4, turn_weight)] + [(0.4, turn_cotangent(i)) for i in range(4)]
    net.spawn(forward(0))
    net.run()

    agg = jnp.concatenate(
        [jnp.concatenate([af[c][e, b] for b in range(4)], axis=1) for e in (0, 1) for c in chunks], axis=0
    )
    pre = dot(wt[...], agg, 1, 0)
    sigma = jax.nn.sigmoid(pre)
    dpre = (cott[...].astype(F32) * sigma * (1.0 + pre * (1.0 - sigma))).astype(BF)
    dagg = dot(wv[...], dpre, 1, 0).astype(BF)
    for e in (0, 1):
        for c in chunks:
            for b in range(4):
                lo = e * TB + offsets[c]
                dall[c][e, b] = dagg[lo:lo + SIZES[c], b * TB:(b + 1) * TB]
    rd = [net.copy(dall[c].at[1 - h], ds[c].at[h], other, "c", bytes_of[c]) for c in chunks]
    for c in chunks:
        ds[c][h] = dall[c][h]
    act_ref[...] = (pre * sigma).astype(BF)
    issued_d = [None] * len(SIZES)

    def backward(c):
        if c:
            for e in issued_d[c - 1]:
                yield e
        yield rd[c]
        events = [along_x[c].gather(PLAN_D[c][g], ds[c].at[g], d_slot(c, g), RANKS[1][0] + c, GATE_D) for g in (0, 1)]
        issued_d[c] = [e[0] for e in events]
        for g in (0, 1):
            dg[c][pl.ds(chip * 8 + g * 4, 4)] = ds[c][g]
        if c == 0:
            wpart[...] = dot(agg, dpre, 1, 1)
            net.now += 0.5
            net.spawn(weights(), 9)
        if c + 1 < len(SIZES):
            net.spawn(backward(c + 1), RANKS[1][0] + c + 1)
        for g in (0, 1):
            yield events[g][1]
        for g in (0, 1):
            multiply(c, g, dg[c], 4, 0)
        dones = [
            along_z[c].scatter(PLAN_B[c][g], backward_part(c, g), bbufs[c][g], fgs[c].at[g], RANKS[1][1] + c)
            for g in (0, 1)
        ]
        for e in dones:
            yield e
        rf = net.copy(fgs[c].at[1 - h], fo[c].at[h], other, "c", bytes_of[c])
        fo[c][h] = fgs[c][h]
        yield rf
        for e in (0, 1):
            lo = e * TB + offsets[c]
            for b in range(4):
                fg_ref[lo:lo + SIZES[c], b * TB:(b + 1) * TB] = fo[c][e, b]

    def weights():
        half = pl.ds(pl.multiple_of(h * TB, TB), TB)
        yield net.copy(wpart.at[pl.ds(pl.multiple_of((1 - h) * TB, TB), TB)], wpair, other, "c", 2**17)
        wpair[...] = wpair[...] + wpart[half]
        own = wpair[pl.ds(pl.multiple_of(row * 8, 8), 8)]
        wrow[row] = own
        cs = [
            net.copy(wpair.at[pl.ds(pl.multiple_of(d[0] * 8, 8), 8)], wrow.at[row], d, "w", 2**13) for d in mates
        ]
        for c in cs:
            yield c
        total = wrow[0]
        for i in range(1, 16):
            total = total + wrow[i]
        wmine[...] = total
        wcol[chip] = total
        cs = [net.copy(wmine, wcol.at[chip], d, "w", 2**13) for d in chips]
        for c in cs:
            yield c
        total = wcol[0]
        for i in range(1, 8):
            total = total + wcol[i]
        here = pl.ds(pl.multiple_of(h * TB + row * 8, 8), 8)
        wfull[here] = total
        cs = [net.copy(wfull.at[here], wfull.at[here], d, "w", 2**13) for d in mates]
        for c in cs:
            yield c
        yield net.copy(wfull.at[half], wfull.at[half], other, "c", 2**17)
        wg_ref[...] = wfull[...]

    net.spawn(backward(0))
    net.run()
    net.finish()


def order_of(targets, sources):
    key = targets * 64 + sources
    rank = jnp.sum((key[None, :] < key[:, None]).astype(jnp.int32), axis=1)
    place = (rank[None, :] == jnp.arange(NT)[:, None]).astype(jnp.int32)
    before = (rank[None, :] == jnp.arange(NT)[:, None] - 1).astype(jnp.int32)
    perm = jnp.sum(place * jnp.arange(NT)[None, :], axis=1)
    source = jnp.sum(place * sources[None, :], axis=1)
    now = jnp.sum(place * targets[None, :], axis=1)
    last = jnp.sum(before * (targets + 1)[None, :], axis=1) - 1
    same = (now == last).astype(jnp.int32)
    blocks = jnp.arange(64)
    upto = jnp.sum((targets[None, :] <= blocks[:, None]).astype(jnp.int32), axis=1)
    found = jnp.max((targets[None, :] == blocks[:, None]).astype(jnp.int32), axis=1)
    wide = lambda v: jnp.pad(v, (0, 128 - v.shape[0]))
    return [wide(perm), wide(source), wide(same), wide(upto * found)]


def turn(act_t, fg_t, wg_in, act_ref, fg_ref, wg_ref):
    for b in range(4):
        here = slice(b * TB, (b + 1) * TB)
        act_ref[here, :] = act_t[:, here].T
        fg_ref[here, :] = fg_t[:, here].T
    wg_ref[...] = wg_in[...]


def body(features, weight, cotangent, tiles, coords):
    rows, cols = coords[0, 0, 0], coords[0, 0, 1]
    idx = jnp.stack(order_of(rows, cols) + order_of(cols, rows)).astype(jnp.int32)
    vmem = pl.BlockSpec(memory_space=pltpu.VMEM)
    hbm = pl.BlockSpec(memory_space=pl.ANY)

    def units(c, *lead):
        return pltpu.VMEM((*lead, 4, SIZES[c], TB), BF)

    def each(*lead):
        return [units(c, *lead) for c in range(len(SIZES))]

    def sums_for(n, plan):
        m = n // 2
        shapes = {"a": ((2, 2, m), (2, 2, m), (), ()), "b": ((2, m), (2, m), (n,), (n,))}
        shapes |= {"e": ((2, n), (2, n), (), ()), "d": ((n,), (n,), (n,), (n,))}
        return [[[units(c, *t) for t in shapes[kind]] for kind in plan[c]] for c in range(len(SIZES))]

    def blocks():
        return [pltpu.VMEM((64, fc, TB), BF) for fc in SIZES]

    act, fg, wg = pl.pallas_call(
        kernel,
        out_shape=(
            jax.ShapeDtypeStruct((256, 512), BF),
            jax.ShapeDtypeStruct((256, 512), BF),
            jax.ShapeDtypeStruct((256, 256), F32),
        ),
        in_specs=[hbm] * 5,
        out_specs=(vmem, vmem, vmem),
        scratch_shapes=[
            pltpu.VMEM((4, TB, 256), BF),
            pltpu.VMEM((256, 256), BF),
            pltpu.VMEM((512, 256), BF),
            pltpu.VMEM((256, 256), BF),
            pltpu.VMEM((256, 512), BF),
            pltpu.VMEM((2, NT, TB, TB), BF),
            pltpu.SMEM((2, 8, TB), jnp.int32),
            each(),
            each(2),
            [list(pair) for pair in zip(blocks(), blocks())],
            [pltpu.VMEM((2 * SLOTS, fc, TB), F32) for fc in SIZES],
            each(2),
            each(2),
            each(2),
            each(2),
            blocks(),
            each(2),
            each(2),
            sums_for(NX, PLAN_F),
            sums_for(NZ, PLAN_B),
            pltpu.VMEM((256, 256), F32),
            pltpu.VMEM((128, 256), F32),
            pltpu.VMEM((16, 8, 256), F32),
            pltpu.VMEM((8, 256), F32),
            pltpu.VMEM((8, 8, 256), F32),
            pltpu.VMEM((256, 256), F32),
            pltpu.SemaphoreType.DMA((5,)),
            pltpu.SemaphoreType.DMA((SEMS,)),
            pltpu.SemaphoreType.DMA((SEMS,)),
        ],
        compiler_params=pltpu.CompilerParams(
            collective_id=0, has_side_effects=True, vmem_limit_bytes=56 * 2**20
        ),
        cost_estimate=pl.CostEstimate(flops=10**9, bytes_accessed=4 * 2**20, transcendentals=2**17),
        name="layer",
    )(features.reshape(4, TB, 256), weight, cotangent, tiles.reshape(NT, TB, TB), idx)
    return pl.pallas_call(
        turn,
        out_shape=(
            jax.ShapeDtypeStruct((512, 256), BF),
            jax.ShapeDtypeStruct((512, 256), BF),
            jax.ShapeDtypeStruct((256, 256), F32),
        ),
        in_specs=[vmem] * 3,
        out_specs=(vmem, vmem, vmem),
        name="turn",
    )(act, fg, wg)


def solution(mesh):
    return jax.shard_map(
        body,
        mesh=mesh,
        in_specs=(
            P(("col", "row"), None),
            P(),
            P(("row", "col"), None),
            P("row", "col", None, None, None),
            P("row", "col", None, None),
        ),
        out_specs=(P(("row", "col"), None), P(("col", "row"), None), P()),
        check_vma=False,
    )
```

time: 675 us -> 136 us (0.20)
  waiting for transfers between devices: 599 us -> 0 us
  Pallas kernels: 0 us -> 134 us
  local copies, waits for them, and re-layouts: 28.1 us -> 1.3 us
  other arithmetic: 22.5 us -> 0.58 us
  between operations: 13.8 us -> 0.75 us
  matrix products: 9.48 us -> 0 us
    psum x1 -> x0, waiting for transfers between devices: 251 us -> none  [body(): weight_grad = lax.psum(partial_weight, ('row', 'col'))]
    reduce_scatter x2 -> x0, waiting for transfers between devices: 213 us -> none  [the longest x1 115 us: body(): lax.psum_scatter(forward, 'col', scatter_dimension=0, tiled=True)]
    all_gather x2 -> x0, waiting for transfers between devices: 135 us -> none  [the longest x1 73 us: body(): lax.all_gather(features, 'row', axis=0, tiled=True)]
    pallas_call x0 -> x2, Pallas kernels: none -> 134 us  [the longest x1 131 us: body(): pl.pallas_call(kernel, out_shape=(jax.ShapeDtypeStruct((256, 512), BF), j...]
    scatter-add x2 -> x0, other arithmetic: 20 us -> none  [advance(): return (carry.at[target_now].add(products), None)]
    dot_general x2 -> x0, local copies, waits for them, and re-layouts: 11.2 us -> none  [the longest x1 5.62 us: advance(): jnp.einsum('gab,gbf->gaf', blocks_now, picked, preferred_element_type=jnp...]
    dot_general x5 -> x0, matrix products: 9.48 us -> none  [the longest x1 2.7 us: advance(): jnp.einsum('gab,gbf->gaf', blocks_now, picked, preferred_element_type=jnp...]
    another operation x2 -> x7, local copies, waits for them, and re-layouts: 8.51 us -> 0.64 us  [body(): jnp.stack(order_of(rows, cols) + order_of(cols, rows)).astype(jnp.int32)]
  transfers between devices with their start and end apart: 5 -> 0, of which waited for: 5 -> 0; matrix products, arithmetic and copies ran while one was open for 1% -> 0% of each run, Pallas kernels for 0% -> 0%
where the time goes in v2:
time: 136 us
  Pallas kernels  134 us (99%)
    pallas_call x1, Pallas kernels, body(): pl.pallas_call(kernel, out_shape=(jax.ShapeDtypeStruct((256, 512), BF), j...  131 us

profile of v2, /device:TPU:1, one launch (start us, length us, event | category | flops | bytes accessed | tf_op | source)
XLA Modules:
  0.0 136.2 jit_solution(3397305631263653289)
XLA Ops:
  0.6 0.0 copy-start
  0.7 0.7 copy-done
  1.3 0.1 convert_reduce_fusion
  1.5 0.2 convert_reduce_fusion.2
  1.7 0.3 select_reduce_fusion
  2.0 0.6 stack.43.idx_hbm
  2.6 131.4 %layer.1 = (bf16[256,512]{1,0:T(8,128)(2,1)}, bf16[256,512]{1,0:T(8,128)(2,1)}, f32[256,256]{1,0:T(8,128)}) custom-call(bf16[4,128,256]{2,1,0:T(8,128)(2,1)} %bitcast.35, bf16[256,256]{1,0:T(8,128)(2,1)} %w_hbm.1, bf16[512,256]{1,0:T(8,128)(2,1)} %cot_hbm.1, bf16[32,128,128]{2,1,0:T(8,128)(2,1)} %bitcast.34, s32[8,128]{1,0:T(8,128)} %stack.43.idx_hbm), custom_call_target="tpu_custom_call" | custom-call | flops 1000000000 | bytes 4194304 | tf_op jit(solution)/shard_map/layer/pallas_call | solution.py:655
  134.0 2.2 %turn.1 = (bf16[512,256]{1,0:T(8,128)(2,1)}, bf16[512,256]{1,0:T(8,128)(2,1)}, f32[256,256]{1,0:T(8,128)}) custom-call(bf16[256,512]{1,0:T(8,128)(2,1)} %get-tuple-element.6.act_t, bf16[256,512]{1,0:T(8,128)(2,1)} %get-tuple-element.7.fg_t, f32[256,256]{1,0:T(8,128)} %get-tuple-element.8.wg_in), custom_call_target="tpu_custom_call" | custom-call | tf_op jit(solution)/shard_map/turn/pallas_call | solution.py:701
  (15 shorter events, 0.1 us)
Async XLA Ops:
  0.6 0.7 copy-start

commit v3 on v2

--- a/solution.py
+++ b/solution.py
@@ -13,11 +13,11 @@
 NZ = 8
 NX = 4
 SLOTS = NT + 1
-SIZES = (64, 64)
+SIZES = (80, 48)
 PLAN_X = ('ab', 'ba')
 PLAN_F = ('aa', 'ab')
-PLAN_D = ('ba', 'aa')
-PLAN_B = ('ab', 'ba')
+PLAN_D = ("de","ee")
+PLAN_B = ('ba', 'ba')
 GATE_X = 2
 GATE_D = 2
 RANKS = ((0, 0), (0, 0))
@@ -266,7 +266,7 @@
                 dst[i] = total.astype(BF)
                 return unused
 
-            lax.fori_loop(lo, lo + cnt, one, 0)
+            lax.fori_loop(lo, lo + cnt, one, 0, unroll=True)
             net.now += 0.05 * cnt
 
         def read(ref):
@@ -421,7 +421,7 @@
     for device in mates + chips + [other]:
         pl.semaphore_signal(barrier, inc=1, device_id=device, device_id_type=MESH)
 
-    pairs = ((x_hbm, xv), (idx_hbm, idx.at[h]), (tiles_hbm, tiles.at[h]), (w_hbm, wv), (cot_hbm, cotv))
+    pairs = ((x_hbm, xv), (idx_hbm, idx.at[0]), (tiles_hbm, tiles.at[0]), (w_hbm, wv), (cot_hbm, cotv))
     loads = [pltpu.make_async_copy(a, b, local.at[i]) for i, (a, b) in enumerate(pairs)]
     for c in loads:
         c.start()
@@ -439,18 +439,20 @@
     for b in range(4):
         block = xv[b, :, mine].T
         for c in chunks:
-            xs[c][h, b] = block[offsets[c]:offsets[c] + SIZES[c]]
+            xs[c][0, b] = block[offsets[c]:offsets[c] + SIZES[c]]
     pl.semaphore_wait(barrier, 23)
 
-    rx = [net.copy(xo[c], xs[c].at[h], other, "c", bytes_of[c]) for c in chunks]
-    ri = net.copy(idx_hbm, idx.at[h], other, "c", 4096)
-    rt = net.copy(tiles_hbm, tiles.at[h], other, "c", 2**20)
+    rx = [net.copy(xo[c], xs[c].at[1], other, "c", bytes_of[c]) for c in chunks]
+    ri = net.copy(idx_hbm, idx.at[1], other, "c", 4096)
+    rt = net.copy(tiles_hbm, tiles.at[1], other, "c", 2**20)
 
     def g_slot(c, g):
         return lambda pp, k, lo, cnt: gs[c][g].at[pl.ds((pp * NZ + k) * 4 + lo, cnt)]
 
+    group = (h, 1 - h)
+
     def d_slot(c, g):
-        return lambda pp, k, lo, cnt: dg[c].at[pl.ds(((k * 2 + pp) * 2 + g) * 4 + lo, cnt)]
+        return lambda pp, k, lo, cnt: dg[c].at[pl.ds(((k * 2 + pp) * 2 + group[g]) * 4 + lo, cnt)]
 
     def multiply(c, g, source, at, side):
         def one(t, unused):
@@ -464,7 +466,7 @@
 
     def forward_part(c, g):
         def part(pp, k, i):
-            at = ((k * 2 + pp) * 2 + g) * 4 + i
+            at = ((k * 2 + pp) * 2 + group[g]) * 4 + i
             return sums[c][idx[0, 3, at]] + sums[c][SLOTS + idx[1, 3, at]]
 
         return part
@@ -478,11 +480,13 @@
         if c:
             for e in issued_x[c - 1]:
                 yield e
-        rx[c].wait()
-        events = [along_z[c].gather(PLAN_X[c][g], xs[c].at[g], g_slot(c, g), RANKS[0][0] + c, GATE_X) for g in (0, 1)]
+        events = []
+        for g in (0, 1):
+            if g == 1:
+                yield rx[c]
+            events.append(along_z[c].gather(PLAN_X[c][g], xs[c].at[g], g_slot(c, g), RANKS[0][0] + c, GATE_X))
+            gs[c][g][pl.ds(row * 4, 4)] = xs[c][g]
         issued_x[c] = [e[0] for e in events]
-        for g in (0, 1):
-            gs[c][g][pl.ds(row * 4, 4)] = xs[c][g]
         if c + 1 < len(SIZES):
             net.spawn(forward(c + 1), RANKS[0][0] + c + 1)
         if c == 0:
@@ -494,13 +498,13 @@
             yield events[g][1]
             multiply(c, g, gs[c][g], 0, 1)
         dones = [
-            along_x[c].scatter(PLAN_F[c][g], forward_part(c, g), fbufs[c][g], aggs[c].at[g], RANKS[0][1] + c)
-            for g in (0, 1)
+            along_x[c].scatter(PLAN_F[c][g], forward_part(c, g), fbufs[c][g], aggs[c].at[g], RANKS[0][1] + c - 0.5 * g)
+            for g in (1, 0)
         ]
-        for e in dones:
-            yield e
-        ra = net.copy(aggs[c].at[1 - h], af[c].at[h], other, "c", bytes_of[c])
-        af[c][h] = aggs[c][h]
+        yield dones[0]
+        ra = net.copy(aggs[c].at[1], af[c].at[h], other, "c", bytes_of[c])
+        yield dones[1]
+        af[c][h] = aggs[c][0]
         yield ra
 
     def turn_weight():
@@ -532,9 +536,9 @@
             for b in range(4):
                 lo = e * TB + offsets[c]
                 dall[c][e, b] = dagg[lo:lo + SIZES[c], b * TB:(b + 1) * TB]
-    rd = [net.copy(dall[c].at[1 - h], ds[c].at[h], other, "c", bytes_of[c]) for c in chunks]
+    rd = [net.copy(dall[c].at[1 - h], ds[c].at[1], other, "c", bytes_of[c]) for c in chunks]
     for c in chunks:
-        ds[c][h] = dall[c][h]
+        ds[c][0] = dall[c][h]
     act_ref[...] = (pre * sigma).astype(BF)
     issued_d = [None] * len(SIZES)
 
@@ -542,11 +546,13 @@
         if c:
             for e in issued_d[c - 1]:
                 yield e
-        yield rd[c]
-        events = [along_x[c].gather(PLAN_D[c][g], ds[c].at[g], d_slot(c, g), RANKS[1][0] + c, GATE_D) for g in (0, 1)]
+        events = []
+        for g in (0, 1):
+            if g == 1:
+                yield rd[c]
+            events.append(along_x[c].gather(PLAN_D[c][g], ds[c].at[g], d_slot(c, g), RANKS[1][0] + c, GATE_D))
+            dg[c][pl.ds(chip * 8 + group[g] * 4, 4)] = ds[c][g]
         issued_d[c] = [e[0] for e in events]
-        for g in (0, 1):
-            dg[c][pl.ds(chip * 8 + g * 4, 4)] = ds[c][g]
         if c == 0:
             wpart[...] = dot(agg, dpre, 1, 1)
             net.now += 0.5
@@ -558,13 +564,13 @@
         for g in (0, 1):
             multiply(c, g, dg[c], 4, 0)
         dones = [
-            along_z[c].scatter(PLAN_B[c][g], backward_part(c, g), bbufs[c][g], fgs[c].at[g], RANKS[1][1] + c)
-            for g in (0, 1)
+            along_z[c].scatter(PLAN_B[c][g], backward_part(c, g), bbufs[c][g], fgs[c].at[g], RANKS[1][1] + c - 0.5 * g)
+            for g in (1, 0)
         ]
-        for e in dones:
-            yield e
-        rf = net.copy(fgs[c].at[1 - h], fo[c].at[h], other, "c", bytes_of[c])
-        fo[c][h] = fgs[c][h]
+        yield dones[0]
+        rf = net.copy(fgs[c].at[1], fo[c].at[h], other, "c", bytes_of[c])
+        yield dones[1]
+        fo[c][h] = fgs[c][0]
         yield rf
         for e in (0, 1):
             lo = e * TB + offsets[c]
@@ -606,21 +612,35 @@
     net.finish()
 
 
-def order_of(targets, sources):
-    key = targets * 64 + sources
-    rank = jnp.sum((key[None, :] < key[:, None]).astype(jnp.int32), axis=1)
-    place = (rank[None, :] == jnp.arange(NT)[:, None]).astype(jnp.int32)
-    before = (rank[None, :] == jnp.arange(NT)[:, None] - 1).astype(jnp.int32)
-    perm = jnp.sum(place * jnp.arange(NT)[None, :], axis=1)
-    source = jnp.sum(place * sources[None, :], axis=1)
-    now = jnp.sum(place * targets[None, :], axis=1)
-    last = jnp.sum(before * (targets + 1)[None, :], axis=1) - 1
-    same = (now == last).astype(jnp.int32)
-    blocks = jnp.arange(64)
-    upto = jnp.sum((targets[None, :] <= blocks[:, None]).astype(jnp.int32), axis=1)
-    found = jnp.max((targets[None, :] == blocks[:, None]).astype(jnp.int32), axis=1)
-    wide = lambda v: jnp.pad(v, (0, 128 - v.shape[0]))
-    return [wide(perm), wide(source), wide(same), wide(upto * found)]
+def write_order(coords_ref, order):
+    i32 = jnp.int32
+    lane = lax.broadcasted_iota(i32, (NT, TB), 1)
+    down = lax.broadcasted_iota(i32, (NT, TB), 0)
+    small = lax.broadcasted_iota(i32, (NT, NT), 1)
+    pick = small == lax.broadcasted_iota(i32, (NT, NT), 0)
+
+    def down_of(values):
+        return jnp.sum(jnp.where(pick, values, 0), axis=1, keepdims=True)
+
+    def along(chosen, values):
+        return jnp.sum(jnp.where(chosen, values, 0), axis=0, keepdims=True)
+
+    lanes = [jnp.broadcast_to(coords_ref[0, 0, i:i + 1, :], (NT, NT)) for i in (0, 1)]
+    downs = [down_of(v) for v in lanes]
+    for at, (a, b) in ((0, (0, 1)), (4, (1, 0))):
+        key = lanes[a] * 64 + lanes[b]
+        target, source = downs[a], downs[b]
+        before = key < target * 64 + source
+        rank = jnp.sum(jnp.where(before, 1, 0), axis=1, keepdims=True)
+        placed = rank == lane
+        now = along(placed, target)
+        last = along(rank == lane - 1, target + 1) - 1
+        order[at:at + 1, :] = along(placed, down)
+        order[at + 1:at + 2, :] = along(placed, source)
+        order[at + 2:at + 3, :] = jnp.where(now == last, 1, 0)
+        upto = along(target <= lane, jnp.ones((NT, TB), i32))
+        found = along(target == lane, jnp.ones((NT, TB), i32))
+        order[at + 3:at + 4, :] = jnp.where(found > 0, upto, 0)
 
 
 def turn(act_t, fg_t, wg_in, act_ref, fg_ref, wg_ref):
@@ -632,10 +652,15 @@
 
 
 def body(features, weight, cotangent, tiles, coords):
-    rows, cols = coords[0, 0, 0], coords[0, 0, 1]
-    idx = jnp.stack(order_of(rows, cols) + order_of(cols, rows)).astype(jnp.int32)
     vmem = pl.BlockSpec(memory_space=pltpu.VMEM)
     hbm = pl.BlockSpec(memory_space=pl.ANY)
+    idx = pl.pallas_call(
+        write_order,
+        out_shape=jax.ShapeDtypeStruct((8, TB), jnp.int32),
+        in_specs=[vmem],
+        out_specs=vmem,
+        name="order",
+    )(coords)
 
     def units(c, *lead):
         return pltpu.VMEM((*lead, 4, SIZES[c], TB), BF)

time: 136 us -> 130 us (0.956)
  Pallas kernels: 134 us -> 130 us
    pallas_call x1, Pallas kernels: 131 us -> 126 us  [body(): pl.pallas_call(kernel, out_shape=(jax.ShapeDtypeStruct((256, 512), BF), j...]
    pallas_call x0 -> x1, Pallas kernels: none -> 1.48 us  [body(): pl.pallas_call(write_order, out_shape=jax.ShapeDtypeStruct((8, TB), jnp.i...]
where the time goes in v3:
time: 130 us
  Pallas kernels  130 us (100%)
    pallas_call x1, Pallas kernels, body(): pl.pallas_call(kernel, out_shape=(jax.ShapeDtypeStruct((256, 512), BF), j...  126 us

profile of v3, /device:TPU:1, one launch (start us, length us, event | category | flops | bytes accessed | tf_op | source)
XLA Modules:
  0.0 130.2 jit_solution(16693633459800413850)
XLA Ops:
  0.6 1.5 %order.1.idx_hbm = s32[8,128]{1,0:T(8,128)} custom-call(s32[1,1,2,32]{3,2,1,0:T(2,128)} %coords_ref.1), custom_call_target="tpu_custom_call" | custom-call | tf_op jit(solution)/shard_map/order/pallas_call | solution.py:657
  2.1 125.9 %layer.1 = (bf16[256,512]{1,0:T(8,128)(2,1)}, bf16[256,512]{1,0:T(8,128)(2,1)}, f32[256,256]{1,0:T(8,128)}) custom-call(bf16[4,128,256]{2,1,0:T(8,128)(2,1)} %bitcast.3, bf16[256,256]{1,0:T(8,128)(2,1)} %w_hbm.1, bf16[512,256]{1,0:T(8,128)(2,1)} %cot_hbm.1, bf16[32,128,128]{2,1,0:T(8,128)(2,1)} %bitcast.2, s32[8,128]{1,0:T(8,128)} %order.1.idx_hbm), custom_call_target="tpu_custom_call" | custom-call | flops 1000000000 | bytes 4194304 | tf_op jit(solution)/shard_map/layer/pallas_call | solution.py:680
  128.1 2.2 %turn.1 = (bf16[512,256]{1,0:T(8,128)(2,1)}, bf16[512,256]{1,0:T(8,128)(2,1)}, f32[256,256]{1,0:T(8,128)}) custom-call(bf16[256,512]{1,0:T(8,128)(2,1)} %get-tuple-element.6.act_t, bf16[256,512]{1,0:T(8,128)(2,1)} %get-tuple-element.7.fg_t, f32[256,256]{1,0:T(8,128)} %get-tuple-element.8.wg_in), custom_call_target="tpu_custom_call" | custom-call | tf_op jit(solution)/shard_map/turn/pallas_call | solution.py:726

commit v4 on v3

--- a/solution.py
+++ b/solution.py
@@ -19,10 +19,15 @@
 PLAN_D = ("de","ee")
 PLAN_B = ('ba', 'ba')
 GATE_X = 2
-GATE_D = 2
+GATE_D = 1
 RANKS = ((0, 0), (0, 0))
 SEMS = 320
 INF = 1e9
+LATE = {"c": 1.5, "y2": 2.7, "x2": 2.7, "w": 8.0, "z": 1.6}
+RATE = 43.0
+EMIT = 0.05
+ISSUE = 0.08
+MULTIPLY = 0.7
 
 
 def dot(a, b, da, db):
@@ -90,14 +95,14 @@
         )
         self.used += 1
         c.start()
-        rate = 400.0 if link == "c" else 43.0
-        late = {"c": 1.0, "y2": 2.7, "x2": 2.7, "w": 8.0}.get(link, 1.6)
+        rate = 400.0 if link == "c" else RATE
+        late = LATE.get(link, LATE["z"])
         names = {"y2": ("y",), "x2": ("x+", "x-")}.get(link, (link,))
         start = max([self.now] + [self.free.get(name, 0.0) for name in names])
         left = start + size / 1000.0 / rate
         for name in names:
             self.free[name] = left
-        self.now += 0.08
+        self.now += ISSUE
         handle = Handle(c, left, left + late)
         self.started.append(handle)
         return handle
@@ -267,7 +272,7 @@
                 return unused
 
             lax.fori_loop(lo, lo + cnt, one, 0, unroll=True)
-            net.now += 0.05 * cnt
+            net.now += EMIT * cnt
 
         def read(ref):
             return lambda i: ref[i].astype(F32)
@@ -462,7 +467,7 @@
             return unused
 
         lax.fori_loop(0, NT, one, 0, unroll=4)
-        net.now += 0.35
+        net.now += MULTIPLY
 
     def forward_part(c, g):
         def part(pp, k, i):

time: 130 us -> 130 us (level)
  no operation moved by 1% of the time
where the time goes in v4:
time: 130 us; the launch traced here: 129 us
  Pallas kernels  129 us (99%)
    pallas_call x1, Pallas kernels, body(): pl.pallas_call(kernel, out_shape=(jax.ShapeDtypeStruct((256, 512), BF), j...  125 us

profile of v4, /device:TPU:1, one launch (start us, length us, event | category | flops | bytes accessed | tf_op | source)
XLA Modules:
  0.0 129.3 jit_solution(7246630129804607678)
XLA Ops:
  0.6 1.5 %order.1.idx_hbm = s32[8,128]{1,0:T(8,128)} custom-call(s32[1,1,2,32]{3,2,1,0:T(2,128)} %coords_ref.1), custom_call_target="tpu_custom_call" | custom-call | tf_op jit(solution)/shard_map/order/pallas_call | solution.py:662
  2.1 125.0 %layer.1 = (bf16[256,512]{1,0:T(8,128)(2,1)}, bf16[256,512]{1,0:T(8,128)(2,1)}, f32[256,256]{1,0:T(8,128)}) custom-call(bf16[4,128,256]{2,1,0:T(8,128)(2,1)} %bitcast.3, bf16[256,256]{1,0:T(8,128)(2,1)} %w_hbm.1, bf16[512,256]{1,0:T(8,128)(2,1)} %cot_hbm.1, bf16[32,128,128]{2,1,0:T(8,128)(2,1)} %bitcast.2, s32[8,128]{1,0:T(8,128)} %order.1.idx_hbm), custom_call_target="tpu_custom_call" | custom-call | flops 1000000000 | bytes 4194304 | tf_op jit(solution)/shard_map/layer/pallas_call | solution.py:685
  127.1 2.2 %turn.1 = (bf16[512,256]{1,0:T(8,128)(2,1)}, bf16[512,256]{1,0:T(8,128)(2,1)}, f32[256,256]{1,0:T(8,128)}) custom-call(bf16[256,512]{1,0:T(8,128)(2,1)} %get-tuple-element.6.act_t, bf16[256,512]{1,0:T(8,128)(2,1)} %get-tuple-element.7.fg_t, f32[256,256]{1,0:T(8,128)} %get-tuple-element.8.wg_in), custom_call_target="tpu_custom_call" | custom-call | tf_op jit(solution)/shard_map/turn/pallas_call | solution.py:731

commit v5 on v4

--- a/solution.py
+++ b/solution.py
@@ -466,7 +466,7 @@
             sums[c][g * SLOTS + 1 + t] = product + keep * sums[c][g * SLOTS + t]
             return unused
 
-        lax.fori_loop(0, NT, one, 0, unroll=4)
+        lax.fori_loop(0, NT, one, 0, unroll=8)
         net.now += MULTIPLY
 
     def forward_part(c, g):

time: 130 us -> 128 us (0.985)
  Pallas kernels: 129 us -> 127 us
    pallas_call x1, Pallas kernels: 125 us -> 124 us  [body(): pl.pallas_call(kernel, out_shape=(jax.ShapeDtypeStruct((256, 512), BF), j...]
where the time goes in v5:
time: 128 us
  Pallas kernels  127 us (99%)
    pallas_call x1, Pallas kernels, body(): pl.pallas_call(kernel, out_shape=(jax.ShapeDtypeStruct((256, 512), BF), j...  124 us

profile of v5, /device:TPU:1, one launch (start us, length us, event | category | flops | bytes accessed | tf_op | source)
XLA Modules:
  0.0 127.8 jit_solution(8757545773725800487)
XLA Ops:
  0.6 1.5 %order.1.idx_hbm = s32[8,128]{1,0:T(8,128)} custom-call(s32[1,1,2,32]{3,2,1,0:T(2,128)} %coords_ref.1), custom_call_target="tpu_custom_call" | custom-call | tf_op jit(solution)/shard_map/order/pallas_call | solution.py:662
  2.1 123.5 %layer.1 = (bf16[256,512]{1,0:T(8,128)(2,1)}, bf16[256,512]{1,0:T(8,128)(2,1)}, f32[256,256]{1,0:T(8,128)}) custom-call(bf16[4,128,256]{2,1,0:T(8,128)(2,1)} %bitcast.3, bf16[256,256]{1,0:T(8,128)(2,1)} %w_hbm.1, bf16[512,256]{1,0:T(8,128)(2,1)} %cot_hbm.1, bf16[32,128,128]{2,1,0:T(8,128)(2,1)} %bitcast.2, s32[8,128]{1,0:T(8,128)} %order.1.idx_hbm), custom_call_target="tpu_custom_call" | custom-call | flops 1000000000 | bytes 4194304 | tf_op jit(solution)/shard_map/layer/pallas_call | solution.py:685
  125.7 2.2 %turn.1 = (bf16[512,256]{1,0:T(8,128)(2,1)}, bf16[512,256]{1,0:T(8,128)(2,1)}, f32[256,256]{1,0:T(8,128)}) custom-call(bf16[256,512]{1,0:T(8,128)(2,1)} %get-tuple-element.6.act_t, bf16[256,512]{1,0:T(8,128)(2,1)} %get-tuple-element.7.fg_t, f32[256,256]{1,0:T(8,128)} %get-tuple-element.8.wg_in), custom_call_target="tpu_custom_call" | custom-call | tf_op jit(solution)/shard_map/turn/pallas_call | solution.py:731
